TPU v7x, 512 devices: a whole 4x8x8 slice. The times are simulated.
512 devices in a mesh: chol: 8 (over x, core), walk: 64 (over y, z).
Axes of the slice: x: 4, y: 8, z: 8, core: 2. Of those that a mesh axis runs over, the one named last changes fastest.
Arguments:
- walkers: float32 [256, 200, 768], P('walk'), may hold values from -6 to 6
- inv_intersection: float32 [256, 2, 100, 100], P('walk'), may hold values from -0.625 to 0.625
- half_vectors: bfloat16 [1024, 200, 768], P('chol', None, 'walk'), may hold values from -0.375 to 0.375
- chol_vectors: bfloat16 [1024, 768, 768], P('chol', 'walk'), may hold values from -0.1875 to 0.1875
- field_draw: float32 [256, 1024], P(None, 'chol'), may hold values from -6 to 6
- counts: int32 [256], replicated, may hold values from 0 to 8, as said below
Outputs:
- new_walkers: float32 [256, 200, 768], P('walk', None, 'chol')
Inputs may be any that keep to these rules, and one draw needn't show every extreme that they name: In each aligned block of 8 walkers the counts sum to 8.
All inputs are finite; a program needn't handle non-finite values.
Results may differ from a plain program's by a relative error of at most 0.024.
Values may be sent and summed in bfloat16 or wider, within the bound.
A program may use at most 64 MiB of HBM per device.

v0:
```python
import jax
import jax.numpy as jnp
from jax import lax
from jax.sharding import PartitionSpec as P

root_step = 0.1


def partner_2(value, axis, distance):
    mask = 2**distance
    pairs = [(source, source ^ mask) for source in range(lax.axis_size(axis))]
    return lax.ppermute(value, axis, pairs)


def inverse_apply(inv_intersection, walkers):
    half_count = inv_intersection.shape[-1]
    spin_up = jnp.einsum(
        "wij,wjk->wik",
        inv_intersection[:, 0],
        walkers[:, :half_count],
        precision=lax.Precision.HIGHEST,
    )
    spin_down = jnp.einsum(
        "wij,wjk->wik",
        inv_intersection[:, 1],
        walkers[:, half_count:],
        precision=lax.Precision.HIGHEST,
    )
    return jnp.concatenate([spin_up, spin_down], axis=1)


def local(walkers, inv_intersection, half_vectors, chol_vectors, field_draw, counts):
    per_device, electrons, orbitals = walkers.shape
    mixed = inverse_apply(inv_intersection, walkers).astype(jnp.bfloat16)
    mixed_rows = lax.all_to_all(mixed, "walk", split_axis=2, concat_axis=0, tiled=True)
    walker_count = mixed_rows.shape[0]
    group_size, _, row_count = half_vectors.shape
    bias_part = lax.dot_general(
        mixed_rows.reshape(walker_count, electrons * row_count),
        half_vectors.reshape(group_size, electrons * row_count),
        (((1,), (1,)), ((), ())),
        preferred_element_type=jnp.float32,
    )
    force_bias = root_step * lax.psum(bias_part, "walk")
    shifted = (field_draw + force_bias).astype(jnp.bfloat16)
    local_rows = chol_vectors.shape[1]
    products = jnp.dot(
        shifted,
        chol_vectors.reshape(group_size, local_rows * orbitals),
        preferred_element_type=jnp.float32,
    )
    partial_value = (root_step * products).astype(jnp.bfloat16)
    partial_value = lax.optimization_barrier(partial_value).reshape(
        walker_count, local_rows, orbitals
    )
    gathered = lax.all_to_all(partial_value, "walk", split_axis=0, concat_axis=1, tiled=True)
    field_rows = lax.psum_scatter(
        gathered.astype(jnp.float32).astype(jnp.bfloat16), "chol", scatter_dimension=1, tiled=True
    )
    row_block = orbitals // lax.axis_size("chol")
    offset = lax.axis_index("chol") * row_block
    own_rows = lax.dynamic_slice_in_dim(walkers, offset, row_block, 2)
    walker_low = walkers.astype(jnp.bfloat16)
    taylor_term = jnp.einsum(
        "wel,wkl->wek", walker_low, field_rows, preferred_element_type=jnp.float32
    )
    summed = own_rows + taylor_term
    for degree in range(2, 5):
        folded = jnp.einsum(
            "wel,wkl->wek",
            lax.all_gather(taylor_term.astype(jnp.bfloat16), "chol", axis=2, tiled=True),
            field_rows,
            preferred_element_type=jnp.float32,
        )
        taylor_term = folded / degree
        summed = summed + taylor_term
    partner = partner_2(summed, "walk", 0)
    lowbit = lax.axis_index("walk") % 2
    leading = jnp.where(lowbit == 0, summed, partner)
    trailing = jnp.where(lowbit == 0, partner, summed)
    pair_block = jnp.concatenate([leading, trailing], axis=0)
    pair_size = 2 * per_device
    block_start = lax.axis_index("walk") // 2 * pair_size
    block_counts = lax.dynamic_slice_in_dim(counts, block_start, pair_size, 0)
    cumulative = jnp.cumsum(block_counts, dtype=jnp.int32)
    slot_index = lowbit * per_device + jnp.arange(per_device, dtype=jnp.int32)
    source = jnp.sum((cumulative[None, :] <= slot_index[:, None]).astype(jnp.int32), axis=1)
    return jnp.take(pair_block, source, axis=0)


def solution(mesh):
    placed = (
        P("walk", None, None),
        P("walk", None, None, None),
        P("chol", None, "walk"),
        P("chol", "walk", None),
        P(None, "chol"),
        P(),
    )
    return jax.shard_map(
        local, mesh=mesh, in_specs=placed, out_specs=P("walk", None, "chol"), check_vma=False
    )
```

profile of v0, /device:TPU:1, one launch (start us, length us, event | category | flops | bytes accessed | tf_op | source)
XLA Modules:
  0.0 631.6 jit_solution(12251369084293642299)
XLA Ops:
  6.5 1.6 fusion.16
  8.2 2.5 convolution_convert_fusion
  10.7 1.2 convolution_convert_fusion.1
  11.9 1.2 pad_maximum_fusion
  13.1 3.7 copy.56
  16.7 17.4 %all-to-all-start = ((bf16[4,200,768]{1,0,2:T(4,128)(2,1)}), bf16[4,200,768]{1,0,2:T(4,128)(2,1)}, u32[]{:S(2)}, u32[]{:S(2)}) async-start(bf16[4,200,768]{1,0,2:T(4,128)(2,1)} %copy.56), calls=%async_computation | async-start | bytes 3145728 | tf_op jit(solution)/shard_map/all_to_all | solution.py:35
  34.2 2.1 copy.58
  36.3 2.0 reshape.62
  38.3 33.3 %all-to-all-done = bf16[4,200,768]{1,0,2:T(4,128)(2,1)} async-done(((bf16[4,200,768]{1,0,2:T(4,128)(2,1)}), bf16[4,200,768]{1,0,2:T(4,128)(2,1)}, u32[]{:S(2)}, u32[]{:S(2)}) %all-to-all-start) | async-done | bytes 1228832 | tf_op jit(solution)/shard_map/all_to_all | solution.py:35
  71.5 10.7 %copy.57 = bf16[64,4,200,12]{3,2,1,0:T(8,128)(2,1)} copy(bf16[64,4,200,12]{2,1,3,0:T(4,128)(2,1)} %bitcast.5) | data formatting | bytes 2457600 | tf_op jit(solution)/shard_map/all_to_all | solution.py:35
  82.3 13.7 %reshape.61 = bf16[256,2400]{1,0:T(8,128)(2,1)} reshape(bf16[64,4,200,12]{3,2,1,0:T(8,128)(2,1)} %copy.57) | data formatting | bytes 2457600 | tf_op jit(solution)/shard_map/reshape | solution.py:39
  96.0 2.6 fusion.20
  98.6 4.3 copy.59
  102.9 142.1 %all-reduce.4.cloned.1.call-done = f32[256,128]{1,0:T(8,128)} async-done(((f32[256,128]{1,0:T(8,128)}), f32[256,128]{1,0:T(8,128)}) %all-reduce.4.cloned.1.call-update) | async-done | bytes 131088 | tf_op jit(solution)/shard_map/psum | solution.py:44
  245.0 5.3 fusion
  250.3 6.7 %copy.60 = bf16[256,9216]{0,1:T(8,128)(2,1)} copy(bf16[256,9216]{1,0:T(8,128)(2,1)} %fusion) | data formatting | bytes 9437184 | tf_op jit(solution)/shard_map/optimization_barrier | solution.py:53
  257.0 8.6 %copy.61 = bf16[256,12,768]{2,1,0:T(8,128)(2,1)} copy(bf16[256,12,768]{0,2,1:T(8,128)(2,1)} %bitcast.38) | data formatting | bytes 9437184 | tf_op jit(solution)/shard_map/reshape | solution.py:53
  265.6 143.7 %all_to_all.33 = bf16[256,12,768]{2,1,0:T(8,128)(2,1)S(1)} all-to-all(bf16[256,12,768]{2,1,0:T(8,128)(2,1)} %copy.61), channel_id=1, replica_groups=mesh['chol'=8,'walk'=64] {'walk'}, dimensions={0} | all-to-all | bytes 9437184 | tf_op jit(solution)/shard_map/all_to_all | solution.py:56
  409.2 4.6 copy.69
  413.9 1.3 dynamic-slice
  415.8 92.4 %all-reduce.6.cloned.1.call-done = bf16[4,768,768]{2,0,1:T(4,128)(2,1)} async-done(((bf16[4,768,768]{2,0,1:T(4,128)(2,1)}), bf16[4,768,768]{2,0,1:T(4,128)(2,1)}) %all-reduce.6.cloned.1.call-update) | async-done | bytes 4718608
  508.2 1.3 constant_dynamic-slice_fusion
  509.5 1.3 fusion.17
  510.9 32.1 %all-gather.4.cloned.1.call-done = bf16[4,200,768]{1,2,0:T(8,128)(2,1)} async-done(((bf16[4,200,96]{1,2,0:T(8,128)(2,1)}), bf16[4,200,768]{1,2,0:T(8,128)(2,1)}) %all-gather.4.cloned.1.call-update) | async-done | bytes 1228816 | tf_op jit(solution)/shard_map/all_gather | solution.py:71
  543.1 2.6 fusion.18
  545.8 30.2 %all-gather.6.cloned.1.call-done = bf16[4,200,768]{1,2,0:T(8,128)(2,1)} async-done(((bf16[4,200,96]{1,2,0:T(8,128)(2,1)}), bf16[4,200,768]{1,2,0:T(8,128)(2,1)}) %all-gather.6.cloned.1.call-update) | async-done | bytes 1228816 | tf_op jit(solution)/shard_map/all_gather | solution.py:71
  575.9 2.6 fusion.19
  579.5 29.4 %all-gather.8.cloned.1.call-done = bf16[4,200,768]{1,2,0:T(8,128)(2,1)} async-done(((bf16[4,200,96]{1,2,0:T(8,128)(2,1)}), bf16[4,200,768]{1,2,0:T(8,128)(2,1)}) %all-gather.8.cloned.1.call-update) | async-done | bytes 1228816 | tf_op jit(solution)/shard_map/all_gather | solution.py:71
  608.8 2.1 fusion.5
  610.9 3.4 collective-permute-start
  614.4 9.1 %collective-permute-done = f32[4,200,96]{1,2,0:T(8,128)S(1)} collective-permute-done((f32[4,200,96]{1,2,0:T(8,128)S(1)}, f32[4,200,96]{1,2,0:T(8,128)S(1)}, u32[]{:S(2)}, u32[]{:S(2)}) %collective-permute-start) | collective-permute-done | bytes 307232 | tf_op jit(solution)/shard_map/ppermute | solution.py:12
  624.2 0.8 broadcast_select_fusion
  (28 shorter events, 1.8 us)
Async XLA Ops:
  6.5 572.5 %copy-start = (s32[256]{0:T(256)S(1)}, s32[256]{0:T(256)}, u32[]{:S(2)}) copy-start(s32[256]{0:T(256)} %param.11) | copy-start | bytes 3076
  6.5 4.2 copy-start.1
  16.7 54.8 %all-to-all-start = ((bf16[4,200,768]{1,0,2:T(4,128)(2,1)}), bf16[4,200,768]{1,0,2:T(4,128)(2,1)}, u32[]{:S(2)}, u32[]{:S(2)}) async-start(bf16[4,200,768]{1,0,2:T(4,128)(2,1)} %copy.56), calls=%async_computation | async-start | bytes 3145728 | tf_op jit(solution)/shard_map/all_to_all | solution.py:35
  34.1 210.9 %all-reduce.4.cloned.1.call-start = ((), (), s32[]{:S(2)}) async-start(), calls=%async_computation.2 | async-start | bytes 262144 | tf_op jit(solution)/shard_map/psum | solution.py:44
  98.6 146.5 %copy-start.2 = (f32[256,128]{1,0:T(8,128)S(1)}, f32[256,128]{1,0:T(8,128)}, u32[]{:S(2)}) copy-start(f32[256,128]{1,0:T(8,128)} %param.10) | copy-start | bytes 393220
  98.6 409.7 %all-reduce.6.cloned.1.call-start = ((), (), s32[]{:S(2)}) async-start(), calls=%async_computation.6 | async-start | bytes 9437184
  413.9 129.2 %all-gather.4.cloned.1.call-start = ((), (), s32[]{:S(2)}) async-start(), calls=%async_computation.3 | async-start | bytes 1769472 | tf_op jit(solution)/shard_map/all_gather | solution.py:71
  510.9 65.1 %all-gather.6.cloned.1.call-start = ((), (), s32[]{:S(2)}) async-start(), calls=%async_computation.4 | async-start | bytes 1769472 | tf_op jit(solution)/shard_map/all_gather | solution.py:71
  545.7 63.1 %all-gather.8.cloned.1.call-start = ((), (), s32[]{:S(2)}) async-start(), calls=%async_computation.5 | async-start | bytes 1769472 | tf_op jit(solution)/shard_map/all_gather | solution.py:71
  610.9 12.5 %collective-permute-start = (f32[4,200,96]{1,2,0:T(8,128)S(1)}, f32[4,200,96]{1,2,0:T(8,128)S(1)}, u32[]{:S(2)}, u32[]{:S(2)}) collective-permute-start(f32[4,200,96]{1,2,0:T(8,128)S(1)} %fusion.5), channel_id=1, source_target_pairs={{0,1},{1,0},{2,3},{3,2},{4,5},{5,4},{6,7},{7,6},{8,9},{9,8},{10,11... | collective-permute-start | bytes 921608 | tf_op jit(solution)/shard_map/ppermute | solution.py:12
Sparse Core Ops, SparseCore 0:
  98.7 146.3 all-reduce.3
  414.0 94.2 all-reduce.5
  511.0 31.9 all-gather.3
  545.8 30.0 all-gather.5
  578.7 30.0 all-gather.7
where the time goes:
time: 633 us; the launch traced here: 632 us
  waiting for transfers between devices  369 us (58%)
  blocking collectives  144 us (23%)
  local copies, waits for them, and re-layouts  61.5 us (10%)
  starting transfers between devices  21 us (3%)
  matrix products  20.3 us (3%)
  between operations  14 us (2%)
    all_to_all x1, blocking collectives, local(): lax.all_to_all(partial_value, 'walk', split_axis=0, concat_axis=1, tiled=...  144 us
    psum x1, waiting for transfers between devices, local(): force_bias = root_step * lax.psum(bias_part, 'walk')  142 us
    unnamed x6, waiting for transfers between devices  92.5 us
    all_gather x3, waiting for transfers between devices, local(): lax.all_gather(taylor_term.astype(jnp.bfloat16), 'chol', axis=2, tiled=True)  91.7 us
    all_to_all x1, waiting for transfers between devices, local(): lax.all_to_all(mixed, 'walk', split_axis=2, concat_axis=0, tiled=True)  33.3 us
    all_to_all x1, starting transfers between devices, local(): lax.all_to_all(mixed, 'walk', split_axis=2, concat_axis=0, tiled=True)  17.4 us
    reshape x1, local copies, waits for them, and re-layouts, local(): mixed_rows.reshape(walker_count, electrons * row_count)  13.7 us
  transfers between devices with their start and end apart: 7, of which 7 were waited for; matrix products, arithmetic and copies ran while one was open for 2% of the time, Pallas kernels for 0%

commit v1 on v0

v1 whole, which is shorter than its diff:
```python
import jax
import jax.numpy as jnp
from jax import lax
from jax.experimental import pallas as pl
from jax.experimental.pallas import tpu as pltpu
from jax.sharding import PartitionSpec as P

root_step = 0.1

NX, NY, NZ = 4, 8, 8
LANES = 128
HALF_E = 100
SHIFT = LANES - HALF_E
M = 768
LH = M // 2
KW = M // (NY * NZ)
XI = KW // NX
WALKERS = NX * NY * NZ
GROUP = 128
COPIES = 160
MESH = pl.DeviceIdType.MESH


def kernel(
    walkers, inverse, half, chol, draw, counts, out,
    wbuf, wt, hbuf, hs, hsend, m1, s1, s1f, s2, mx, mbig, fsend, fown, frecv, fz, fr, fy, fyr,
    drawbuf, sg, cr, pz, rz, qx, rx, gbuf, qy, fb, cur, prop, cand, ssem, rsem, lsem,
):
    c = lax.axis_index("chol")
    w = lax.axis_index("walk")
    x = lax.div(c, 2)
    core = lax.rem(c, 2)
    y = lax.div(w, NZ)
    z = lax.rem(w, NZ)
    other = 1 - core
    partner_w = w + 1 - 2 * lax.rem(w, 2)

    def at_y(d):
        t = lax.rem(y + d, NY)
        return t, (c, t * NZ + z)

    def at_z(d):
        t = lax.rem(z + d, NZ)
        return t, (c, y * NZ + t)

    def at_x(d):
        t = lax.rem(x + d, NX)
        return t, (t * 2 + core, w)

    mate = (x * 2 + other, w)

    barrier = pltpu.get_barrier_semaphore()
    greeted = 0
    peers = [at_y(d)[1] for d in range(1, NY)] + [at_z(d)[1] for d in range(1, NZ)]
    finals = []
    for dx in range(NX):
        for dc in range(2):
            tx = lax.rem(x + dx, NX)
            tc = tx * 2 + (core if dc == 0 else other)
            for dp in range(2):
                if dx or dc or dp:
                    finals.append((dx, dc, dp, tc, (tc, partner_w if dp else w)))
                    if dx or dc:
                        peers.append((tc, partner_w if dp else w))
    for peer in peers:
        pl.semaphore_signal(barrier, inc=1, device_id=peer, device_id_type=MESH)
        greeted += 1

    started = []

    def send(src, dst, device):
        i = len(started)
        copy = pltpu.make_async_remote_copy(
            src_ref=src, dst_ref=dst, send_sem=ssem.at[i], recv_sem=rsem.at[i],
            device_id=device, device_id_type=MESH,
        )
        copy.start()
        started.append(copy)
        return copy

    load_w = pltpu.make_async_copy(walkers.at[x], wbuf, lsem.at[0])
    load_h = pltpu.make_async_copy(half, hbuf, lsem.at[1])
    load_d = pltpu.make_async_copy(draw, drawbuf, lsem.at[2])
    load_c = pltpu.make_async_copy(
        chol.at[pl.ds(XI * x, XI), :, pl.ds(pl.multiple_of(LH * core, LANES), LH)], cr.at[c], lsem.at[3]
    )
    load_w.start()
    load_h.start()
    load_d.start()
    load_c.start()

    load_w.wait()
    electron = lax.broadcasted_iota(jnp.int32, (LANES, M), 0)
    up = jnp.where(electron < HALF_E, wbuf[0:LANES, :], 0.0)
    down = jnp.where(electron >= SHIFT, wbuf[2 * HALF_E - LANES : 2 * HALF_E, :], 0.0)
    wt[...] = jnp.where(core == 0, up, down).T
    mixed = lax.dot_general(
        wt[...], inverse[...], (((1,), (1,)), ((), ())),
        precision=lax.Precision.HIGHEST, preferred_element_type=jnp.float32,
    )
    m1[...] = mixed.astype(jnp.bfloat16).reshape(NY, M // NY, LANES)
    s1[y] = m1[y]

    pl.semaphore_wait(barrier, greeted)

    copies = []
    for d in range(1, NY):
        t, device = at_y(d)
        copies.append(send(m1.at[t], s1.at[y], device))

    chol_copies = []
    for dx in range(NX):
        for dc in range(2):
            if dx or dc:
                tx = lax.rem(x + dx, NX)
                tcore = core if dc == 0 else other
                chol_copies.append(
                    send(
                        chol.at[pl.ds(XI * tx, XI), :, pl.ds(pl.multiple_of(LH * tcore, LANES), LH)],
                        cr.at[c],
                        (tx * 2 + tcore, w),
                    )
                )

    load_h.wait()
    for k in range(KW):
        rows = hbuf[k].astype(jnp.float32)
        first = rows[0:LANES]
        second = rows[2 * HALF_E - LANES : 2 * HALF_E]
        hs[core, LANES * k : LANES * (k + 1)] = jnp.where(core == 0, first, second).astype(jnp.bfloat16)
        hsend[LANES * k : LANES * (k + 1)] = jnp.where(core == 0, second, first).astype(jnp.bfloat16)
    half_copy = send(hsend, hs.at[core], mate)

    for copy in copies:
        copy.wait_recv()

    rows_y = M // NY
    for t in range(NY):
        s1f[rows_y * t : rows_y * (t + 1)] = s1[t].astype(jnp.float32)

    @pl.loop(0, NZ)
    def _(t):
        for p in range(KW // 2):
            pair = [s1f[pl.ds(KW * t + 2 * p + q, NY, stride=rows_y), :] for q in range(2)]
            s2[t, 16 * p : 16 * (p + 1)] = jnp.concatenate(pair, axis=0).astype(jnp.bfloat16)

    mx[x, z] = s2[z]
    copies = []
    for d in range(1, NZ):
        t, device = at_z(d)
        copies.append(send(s2.at[t], mx.at[x, z], device))
    for copy in copies:
        copy.wait_recv()

    copies = []
    for d in range(1, NX):
        copies.append(send(mx.at[x], mx.at[x], at_x(d)[1]))
    for copy in copies:
        copy.wait_recv()

    @pl.loop(0, NZ)
    def _(t):
        for p in range(KW // 2):
            blocks = [mx[q, t, 16 * p : 16 * (p + 1)].astype(jnp.float32) for q in range(NX)]
            for q in range(2):
                rows = jnp.concatenate([b[8 * q : 8 * (q + 1)] for b in blocks], axis=0)
                k = 2 * p + q
                mbig[t, :, LANES * k : LANES * (k + 1)] = rows.astype(jnp.bfloat16)

    half_copy.wait_recv()
    vectors = jnp.concatenate([hs[0], hs[1]], axis=1)
    bias = jnp.dot(
        mbig[...].reshape(WALKERS, KW * LANES), vectors, preferred_element_type=jnp.float32
    )
    low, high = bias[:, :GROUP], bias[:, GROUP:]
    fown[...] = jnp.where(core == 0, low, high)
    fsend[...] = jnp.where(core == 0, high, low)
    spin_copy = send(fsend, frecv, mate)
    spin_copy.wait_recv()
    fz[...] = (fown[...] + frecv[...]).reshape(NZ, WALKERS // NZ, GROUP)

    fr[z] = fz[z]
    copies = []
    for d in range(1, NZ):
        t, device = at_z(d)
        copies.append(send(fz.at[t], fr.at[z], device))
    for copy in copies:
        copy.wait_recv()
    fy[...] = jnp.sum(fr[...], axis=0)
    fyr[y] = fy[...]
    copies = []
    for d in range(1, NY):
        t, device = at_y(d)
        copies.append(send(fy, fyr.at[y], device))
    load_d.wait()
    own_draw = jnp.concatenate(
        [drawbuf[pl.ds(NX * z + q, NY, stride=NX * NZ), :] for q in range(NX)], axis=0
    )
    for copy in copies:
        copy.wait_recv()
    total = jnp.sum(fyr[...], axis=0)
    sg[c, z] = (own_draw + root_step * total).astype(jnp.bfloat16)

    copies = []
    for d in range(1, NZ):
        t, device = at_z(d)
        copies.append(send(sg.at[c, z], sg.at[c, z], device))
    for copy in copies:
        copy.wait_recv()
    copies = []
    for d in range(1, NX):
        copies.append(send(sg.at[c], sg.at[c], at_x(d)[1]))
    mate_copies = [send(sg.at[c], sg.at[c], mate)]
    for d, copy in enumerate(copies, 1):
        copy.wait_recv()
        source = lax.rem(x - d + NX, NX) * 2 + core
        mate_copies.append(send(sg.at[source], sg.at[source], mate))
    for copy in mate_copies:
        copy.wait_recv()
    load_c.wait()
    for copy in chol_copies:
        copy.wait_recv()

    shifted = jnp.concatenate([sg[g].reshape(WALKERS, GROUP) for g in range(2 * NX)], axis=1)
    block = WALKERS // NZ
    for i in range(XI):
        columns = cr[:, i].reshape(2 * NX * GROUP, LH)
        product = jnp.dot(shifted, columns, preferred_element_type=jnp.float32)
        product = (root_step * product).astype(jnp.bfloat16)
        pz[:, block * i : block * (i + 1), :] = product.reshape(NZ, block, LH)

    rz[z] = pz[z]
    copies = []
    for d in range(1, NZ):
        t, device = at_z(d)
        copies.append(send(pz.at[t], rz.at[z], device))
    for copy in copies:
        copy.wait_recv()

    @pl.loop(0, NZ // 2)
    def _(pair):
        tiles = []
        for t in range(2):
            for i in range(XI):
                tiles.append(rz[2 * pair + t, block * i : block * (i + 1), :].astype(jnp.float32))
        for p in range(XI):
            for q in range(NX):
                two = [tiles[2 * p + r][8 * q : 8 * (q + 1)] for r in range(2)]
                start = pl.multiple_of(2 * XI * NY * pair + 16 * p, 16)
                qx[q, pl.ds(start, 16), :] = jnp.concatenate(two, axis=0).astype(jnp.bfloat16)

    rx[x] = qx[x]
    copies = []
    for d in range(1, NX):
        t, device = at_x(d)
        copies.append(send(qx.at[t], rx.at[x], device))
    for copy in copies:
        copy.wait_recv()

    run = XI * NY

    @pl.loop(0, NZ // 2)
    def _(pair):
        for q in range(NX):
            rows = rx[q, pl.ds(pl.multiple_of(2 * run * pair, 16), 2 * run), :].astype(jnp.float32)
            for t in range(2):
                start = pl.multiple_of((2 * NX * pair + NX * t + q) * run, 8)
                for v in range(LH // LANES):
                    gbuf[v, pl.ds(start, run), :] = rows[run * t : run * (t + 1), LANES * v : LANES * (v + 1)]

    @pl.loop(0, NY)
    def _(t):
        for v in range(LH // LANES):
            for r in range(rows_y // 16):
                two = [gbuf[v, pl.ds((16 * r + 8 * q) * NY + t, 8, stride=NY), :] for q in range(2)]
                qy[t, 16 * r : 16 * (r + 1), LANES * v : LANES * (v + 1)] = jnp.concatenate(
                    two, axis=0
                ).astype(jnp.bfloat16)

    fb[core, y] = qy[y]
    copies = []
    for d in range(1, NY):
        t, device = at_y(d)
        copies.append(send(qy.at[t], fb.at[core, y], device))
    mate_copies = [send(fb.at[core, y], fb.at[core, y], mate)]
    for d, copy in enumerate(copies, 1):
        copy.wait_recv()
        source = lax.rem(y - d + NY, NY)
        mate_copies.append(send(fb.at[core, source], fb.at[core, source], mate))
    for copy in mate_copies:
        copy.wait_recv()

    cur[...] = wt[...].astype(jnp.bfloat16)
    prop[...] = wt[...]
    for degree in range(1, 5):
        field = jnp.concatenate([fb[0].reshape(M, LH), fb[1].reshape(M, LH)], axis=1)
        term = jnp.dot(field, cur[...], preferred_element_type=jnp.float32)
        if degree > 1:
            term = term / degree
        prop[...] += term
        if degree < 4:
            cur[...] = term.astype(jnp.bfloat16)

    rows_c = M // (2 * NX)
    copies = []
    own_slot = lax.rem(w, 2) * NX + x
    for dx, dc, dp, tc, device in finals:
        start = pl.multiple_of(rows_c * tc, 8)
        copies.append(send(prop.at[pl.ds(start, rows_c)], cand.at[own_slot, core], device))
    cand[own_slot, core] = prop[pl.ds(pl.multiple_of(rows_c * c, 8), rows_c), :]

    first = lax.div(w, 2) * (2 * NX)
    sums = counts[first]
    source = [jnp.int32(0)] * NX
    for i in range(2 * NX):
        if i:
            sums = sums + counts[first + i]
        for j in range(NX):
            source[j] = source[j] + jnp.where(sums <= lax.rem(w, 2) * NX + j, 1, 0)
    source = [jnp.minimum(s, 2 * NX - 1) for s in source]
    for copy in copies:
        copy.wait_recv()
    lane = lax.broadcasted_iota(jnp.int32, (rows_c, LANES), 1)
    for j in range(NX):
        up = cand[source[j], 0]
        down = pltpu.roll(cand[source[j], 1], HALF_E - SHIFT, 1)
        out[j, :, 0:LANES] = jnp.where(lane < HALF_E, up, down)
        out[j, :, LANES : 2 * HALF_E] = down[:, : 2 * HALF_E - LANES]

    for copy in started:
        copy.wait_send()


def local(walkers, inv_intersection, half_vectors, chol_vectors, field_draw, counts):
    c = lax.axis_index("chol")
    x, core = c // 2, c % 2
    own = lax.dynamic_index_in_dim(inv_intersection, x, 0, keepdims=False)
    padded = jnp.pad(own, ((0, 0), (SHIFT, SHIFT), (SHIFT, SHIFT)))
    inverse = jnp.where(core == 0, padded[0, SHIFT:, SHIFT:], padded[1, :LANES, :LANES])
    half = half_vectors.transpose(2, 1, 0)
    chol = chol_vectors.transpose(1, 0, 2)
    f32, bf16 = jnp.float32, jnp.bfloat16
    rows_y, rows_c, block = M // NY, M // (2 * NX), WALKERS // NZ
    vmem = pltpu.VMEM
    scratch = dict(
        wbuf=vmem((2 * HALF_E, M), f32),
        wt=vmem((M, LANES), f32),
        hbuf=vmem((KW, 2 * HALF_E, GROUP), bf16),
        hs=vmem((2, KW * LANES, GROUP), bf16),
        hsend=vmem((KW * LANES, GROUP), bf16),
        m1=vmem((NY, rows_y, LANES), bf16),
        s1=vmem((NY, rows_y, LANES), bf16),
        s1f=vmem((NY * rows_y, LANES), f32),
        s2=vmem((NZ, KW * NY, LANES), bf16),
        mx=vmem((NX, NZ, KW * NY, LANES), bf16),
        mbig=vmem((NZ, block, KW * LANES), bf16),
        fsend=vmem((WALKERS, GROUP), f32),
        fown=vmem((WALKERS, GROUP), f32),
        frecv=vmem((WALKERS, GROUP), f32),
        fz=vmem((NZ, block, GROUP), f32),
        fr=vmem((NZ, block, GROUP), f32),
        fy=vmem((block, GROUP), f32),
        fyr=vmem((NY, block, GROUP), f32),
        drawbuf=vmem((WALKERS, GROUP), f32),
        sg=vmem((2 * NX, NZ, block, GROUP), bf16),
        cr=vmem((2 * NX, XI, GROUP, LH), bf16),
        pz=vmem((NZ, XI * block, LH), bf16),
        rz=vmem((NZ, XI * block, LH), bf16),
        qx=vmem((NX, NZ * XI * NY, LH), bf16),
        rx=vmem((NX, NZ * XI * NY, LH), bf16),
        gbuf=vmem((LH // LANES, NZ * NX * XI * NY, LANES), f32),
        qy=vmem((NY, rows_y, LH), bf16),
        fb=vmem((2, NY, rows_y, LH), bf16),
        cur=vmem((M, LANES), bf16),
        prop=vmem((M, LANES), f32),
        cand=vmem((2 * NX, 2, rows_c, LANES), f32),
        ssem=pltpu.SemaphoreType.DMA((COPIES,)),
        rsem=pltpu.SemaphoreType.DMA((COPIES,)),
        lsem=pltpu.SemaphoreType.DMA((4,)),
    )
    hbm = pl.BlockSpec(memory_space=pltpu.HBM)
    in_vmem = pl.BlockSpec(memory_space=pltpu.VMEM)
    in_smem = pl.BlockSpec(memory_space=pltpu.SMEM)
    result = pl.pallas_call(
        kernel,
        out_shape=jax.ShapeDtypeStruct((NX, rows_c, 2 * HALF_E), f32),
        in_specs=[hbm, in_vmem, hbm, hbm, hbm, in_smem],
        out_specs=in_vmem,
        scratch_shapes=list(scratch.values()),
        compiler_params=pltpu.CompilerParams(
            collective_id=0, has_side_effects=True, vmem_limit_bytes=48 * 2**20
        ),
    )(walkers, inverse, half, chol, field_draw, counts)
    return result.transpose(0, 2, 1)


def solution(mesh):
    placed = (
        P("walk", None, None),
        P("walk", None, None, None),
        P("chol", None, "walk"),
        P("chol", "walk", None),
        P(None, "chol"),
        P(),
    )
    return jax.shard_map(
        local, mesh=mesh, in_specs=placed, out_specs=P("walk", None, "chol"), check_vma=False
    )
```

time: 633 us -> 141 us (0.22)
  waiting for transfers between devices: 369 us -> 0 us
  blocking collectives: 144 us -> 0 us
  Pallas kernels: 0 us -> 133 us
  local copies, waits for them, and re-layouts: 61.5 us -> 7.78 us
  starting transfers between devices: 21 us -> 0 us
  matrix products: 20.3 us -> 0 us
  between operations: 14 us -> 0.04 us
    all_to_all x1 -> x0, blocking collectives: 144 us -> none  [local(): lax.all_to_all(partial_value, 'walk', split_axis=0, concat_axis=1, tiled=...]
    psum x1 -> x0, waiting for transfers between devices: 142 us -> none  [local(): force_bias = root_step * lax.psum(bias_part, 'walk')]
    pallas_call x0 -> x1, Pallas kernels: none -> 133 us  [local(): pl.pallas_call(kernel, out_shape=jax.ShapeDtypeStruct((NX, rows_c, 2 * HA...]
    unnamed x6 -> x0, waiting for transfers between devices: 92.5 us -> none
    all_gather x3 -> x0, waiting for transfers between devices: 91.7 us -> none  [local(): lax.all_gather(taylor_term.astype(jnp.bfloat16), 'chol', axis=2, tiled=True)]
    all_to_all x1 -> x0, waiting for transfers between devices: 33.3 us -> none  [local(): lax.all_to_all(mixed, 'walk', split_axis=2, concat_axis=0, tiled=True)]
    reshape x3 -> x0, local copies, waits for them, and re-layouts: 24.2 us -> none  [the longest x1 13.7 us: local(): mixed_rows.reshape(walker_count, electrons * row_count)]
    dot_general x8 -> x0, matrix products: 20.3 us -> none  [the longest x3 7.35 us: local(): jnp.einsum('wel,wkl->wek', lax.all_gather(taylor_term.astype(jnp.bfloat16...]
  transfers between devices with their start and end apart: 7 -> 0, of which waited for: 7 -> 0; matrix products, arithmetic and copies ran while one was open for 2% -> 0% of each run, Pallas kernels for 0% -> 0%
where the time goes in v1:
time: 141 us
  Pallas kernels  133 us (94%)
  local copies, waits for them, and re-layouts  7.78 us (6%)
    pallas_call x1, Pallas kernels, local(): pl.pallas_call(kernel, out_shape=jax.ShapeDtypeStruct((NX, rows_c, 2 * HA...  133 us
    unnamed x13, local copies, waits for them, and re-layouts  7.76 us

profile of v1, /device:TPU:1, one launch (start us, length us, event | category | flops | bytes accessed | tf_op | source)
XLA Modules:
  0.0 140.8 jit_solution(352301352498629966)
XLA Ops:
  0.0 0.0 copy-start
  0.0 1.0 copy-done
  1.0 0.1 fusion.1.inverse
  1.1 0.0 copy-start.1
  1.1 1.7 %copy-done.1 = f32[4,200,768]{2,1,0:T(8,128)S(1)} copy-done((f32[4,200,768]{2,1,0:T(8,128)S(1)}, f32[4,200,768]{2,1,0:T(8,128)}, u32[]{:S(2)}) %copy-start.1) | copy-done | bytes 2457624
  2.8 0.0 copy-start.2
  2.8 1.7 %copy-done.2 = bf16[128,12,768]{2,0,1:T(8,128)(2,1)S(1)} copy-done((bf16[128,12,768]{2,0,1:T(8,128)(2,1)S(1)}, bf16[128,12,768]{2,0,1:T(8,128)(2,1)}, u32[]{:S(2)}) %copy-start.2) | copy-done | bytes 2359320
  4.5 0.0 copy-start.3
  4.5 1.1 copy-done.3
  5.6 0.0 copy-start.4
  5.6 0.9 copy-done.4
  6.5 0.0 copy-start.5
  6.5 0.7 copy-done.5
  7.1 132.9 %shard_map.64 = f32[4,96,200]{2,1,0:T(8,128)S(1)} custom-call(f32[4,200,768]{2,1,0:T(8,128)S(1)} %copy-done.1, f32[128,128]{1,0:T(8,128)S(1)} %fusion.1.inverse, bf16[12,200,128]{2,1,0:T(8,128)(2,1)S(1)} %bitcast.10, bf16[12,128,768]{2,1,0:T(8,128)(2,1)S(1)} %bitcast.8, f32[256,128]{1,0:T(8,128)S(1)} %copy-done.4, s32[256]{0:T(256)S(1)} %copy-done.5), custom_call_target="tpu_custom_call" | custom-call | tf_op jit(solution)/shard_map/pallas_call | solution.py:384
  140.1 0.7 copy.11
  (2 shorter events, 0.0 us)
Async XLA Ops:
  0.0 1.0 copy-start
  1.1 1.7 %copy-start.1 = (f32[4,200,768]{2,1,0:T(8,128)S(1)}, f32[4,200,768]{2,1,0:T(8,128)}, u32[]{:S(2)}) copy-start(f32[4,200,768]{2,1,0:T(8,128)} %walkers.1) | copy-start | bytes 7372804
  2.8 1.7 %copy-start.2 = (bf16[128,12,768]{2,0,1:T(8,128)(2,1)S(1)}, bf16[128,12,768]{2,0,1:T(8,128)(2,1)}, u32[]{:S(2)}) copy-start(bf16[128,12,768]{2,0,1:T(8,128)(2,1)} %param.9) | copy-start | bytes 7077892
  4.5 1.1 copy-start.3
  5.6 0.9 copy-start.4
  6.5 0.7 copy-start.5

commit v2 on v1

--- a/solution.py
+++ b/solution.py
@@ -17,14 +17,14 @@
 XI = KW // NX
 WALKERS = NX * NY * NZ
 GROUP = 128
-COPIES = 160
+COPIES = 256
 MESH = pl.DeviceIdType.MESH
 
 
 def kernel(
     walkers, inverse, half, chol, draw, counts, out,
-    wbuf, wt, hbuf, hs, hsend, m1, s1, s1f, s2, mx, mbig, fsend, fown, frecv, fz, fr, fy, fyr,
-    drawbuf, sg, cr, pz, rz, qx, rx, gbuf, qy, fb, cur, prop, cand, ssem, rsem, lsem,
+    wbuf, wt, hbuf, hs, hsend, m1, s1, s1f, s2, mx, mbig, fz, fr, fy, fyr,
+    drawbuf, sg, cr, pz, rz, qx, rx, gbuf, qy, fb, cur, prop, low, cand, ssem, rsem, lsem,
 ):
     c = lax.axis_index("chol")
     w = lax.axis_index("walk")
@@ -109,18 +109,19 @@
         copies.append(send(m1.at[t], s1.at[y], device))
 
     chol_copies = []
-    for dx in range(NX):
-        for dc in range(2):
-            if dx or dc:
-                tx = lax.rem(x + dx, NX)
-                tcore = core if dc == 0 else other
-                chol_copies.append(
-                    send(
-                        chol.at[pl.ds(XI * tx, XI), :, pl.ds(pl.multiple_of(LH * tcore, LANES), LH)],
-                        cr.at[c],
-                        (tx * 2 + tcore, w),
+
+    def send_chol(distances):
+        for dx in distances:
+            for dc in range(2):
+                if dx or dc:
+                    tx = lax.rem(x + dx, NX)
+                    tcore = core if dc == 0 else other
+                    columns = pl.ds(pl.multiple_of(LH * tcore, LANES), LH)
+                    chol_copies.append(
+                        send(chol.at[pl.ds(XI * tx, XI), :, columns], cr.at[c], (tx * 2 + tcore, w))
                     )
-                )
+
+    send_chol((0, 1, NX - 1))
 
     load_h.wait()
     for k in range(KW):
@@ -149,14 +150,17 @@
     for d in range(1, NZ):
         t, device = at_z(d)
         copies.append(send(s2.at[t], mx.at[x, z], device))
-    for copy in copies:
-        copy.wait_recv()
-
-    copies = []
-    for d in range(1, NX):
-        copies.append(send(mx.at[x], mx.at[x], at_x(d)[1]))
-    for copy in copies:
-        copy.wait_recv()
+
+    x_copies = []
+    for d in range(NZ):
+        if d:
+            copies[d - 1].wait_recv()
+        source = lax.rem(z - d + NZ, NZ)
+        for e in range(1, NX):
+            x_copies.append(send(mx.at[x, source], mx.at[x, source], at_x(e)[1]))
+    for copy in x_copies:
+        copy.wait_recv()
+    send_chol(range(2, NX - 1))
 
     @pl.loop(0, NZ)
     def _(t):
@@ -172,21 +176,19 @@
     bias = jnp.dot(
         mbig[...].reshape(WALKERS, KW * LANES), vectors, preferred_element_type=jnp.float32
     )
-    low, high = bias[:, :GROUP], bias[:, GROUP:]
-    fown[...] = jnp.where(core == 0, low, high)
-    fsend[...] = jnp.where(core == 0, high, low)
-    spin_copy = send(fsend, frecv, mate)
-    spin_copy.wait_recv()
-    fz[...] = (fown[...] + frecv[...]).reshape(NZ, WALKERS // NZ, GROUP)
-
-    fr[z] = fz[z]
-    copies = []
-    for d in range(1, NZ):
-        t, device = at_z(d)
-        copies.append(send(fz.at[t], fr.at[z], device))
+    for q in range(2):
+        part = bias[:, GROUP * q : GROUP * (q + 1)].astype(jnp.bfloat16)
+        fz[q] = part.reshape(NZ, WALKERS // NZ, GROUP)
+
+    fr[core, z] = fz[core, z]
+    copies = []
+    for d in range(NZ):
+        t, _ = at_z(d)
+        for tcore in (core, other) if d else (other,):
+            copies.append(send(fz.at[tcore, t], fr.at[core, z], (x * 2 + tcore, y * NZ + t)))
     for copy in copies:
         copy.wait_recv()
-    fy[...] = jnp.sum(fr[...], axis=0)
+    fy[...] = jnp.sum(fr[...].astype(jnp.float32), axis=(0, 1)).astype(jnp.bfloat16)
     fyr[y] = fy[...]
     copies = []
     for d in range(1, NY):
@@ -198,7 +200,7 @@
     )
     for copy in copies:
         copy.wait_recv()
-    total = jnp.sum(fyr[...], axis=0)
+    total = jnp.sum(fyr[...].astype(jnp.float32), axis=0)
     sg[c, z] = (own_draw + root_step * total).astype(jnp.bfloat16)
 
     copies = []
@@ -223,77 +225,95 @@
 
     shifted = jnp.concatenate([sg[g].reshape(WALKERS, GROUP) for g in range(2 * NX)], axis=1)
     block = WALKERS // NZ
-    for i in range(XI):
-        columns = cr[:, i].reshape(2 * NX * GROUP, LH)
-        product = jnp.dot(shifted, columns, preferred_element_type=jnp.float32)
-        product = (root_step * product).astype(jnp.bfloat16)
-        pz[:, block * i : block * (i + 1), :] = product.reshape(NZ, block, LH)
-
-    rz[z] = pz[z]
-    copies = []
-    for d in range(1, NZ):
-        t, device = at_z(d)
-        copies.append(send(pz.at[t], rz.at[z], device))
-    for copy in copies:
-        copy.wait_recv()
-
-    @pl.loop(0, NZ // 2)
-    def _(pair):
-        tiles = []
-        for t in range(2):
-            for i in range(XI):
-                tiles.append(rz[2 * pair + t, block * i : block * (i + 1), :].astype(jnp.float32))
-        for p in range(XI):
+    run = XI * NY
+
+    def to_z(v):
+        for i in range(XI):
+            columns = cr[:, i, :, LANES * v : LANES * (v + 1)].reshape(2 * NX * GROUP, LANES)
+            product = jnp.dot(shifted, columns, preferred_element_type=jnp.float32)
+            product = (root_step * product).astype(jnp.bfloat16)
+            pz[v, :, block * i : block * (i + 1), :] = product.reshape(NZ, block, LANES)
+        rz[v, z] = pz[v, z]
+        copies = []
+        for d in range(1, NZ):
+            t, device = at_z(d)
+            copies.append(send(pz.at[v, t], rz.at[v, z], device))
+        return copies
+
+    def to_x(v):
+        @pl.loop(0, NZ // 2)
+        def _(pair):
+            tiles = []
+            for t in range(2):
+                for i in range(XI):
+                    tiles.append(rz[v, 2 * pair + t, block * i : block * (i + 1), :].astype(jnp.float32))
+            for p in range(XI):
+                for q in range(NX):
+                    two = [tiles[2 * p + r][8 * q : 8 * (q + 1)] for r in range(2)]
+                    start = pl.multiple_of(2 * run * pair + 16 * p, 16)
+                    qx[v, q, pl.ds(start, 16), :] = jnp.concatenate(two, axis=0).astype(jnp.bfloat16)
+
+        rx[v, x] = qx[v, x]
+        copies = []
+        for d in range(1, NX):
+            t, device = at_x(d)
+            copies.append(send(qx.at[v, t], rx.at[v, x], device))
+        return copies
+
+    def to_y(v):
+        @pl.loop(0, NZ // 2)
+        def _(pair):
             for q in range(NX):
-                two = [tiles[2 * p + r][8 * q : 8 * (q + 1)] for r in range(2)]
-                start = pl.multiple_of(2 * XI * NY * pair + 16 * p, 16)
-                qx[q, pl.ds(start, 16), :] = jnp.concatenate(two, axis=0).astype(jnp.bfloat16)
-
-    rx[x] = qx[x]
-    copies = []
-    for d in range(1, NX):
-        t, device = at_x(d)
-        copies.append(send(qx.at[t], rx.at[x], device))
-    for copy in copies:
-        copy.wait_recv()
-
-    run = XI * NY
-
-    @pl.loop(0, NZ // 2)
-    def _(pair):
-        for q in range(NX):
-            rows = rx[q, pl.ds(pl.multiple_of(2 * run * pair, 16), 2 * run), :].astype(jnp.float32)
-            for t in range(2):
-                start = pl.multiple_of((2 * NX * pair + NX * t + q) * run, 8)
-                for v in range(LH // LANES):
-                    gbuf[v, pl.ds(start, run), :] = rows[run * t : run * (t + 1), LANES * v : LANES * (v + 1)]
-
-    @pl.loop(0, NY)
-    def _(t):
-        for v in range(LH // LANES):
+                rows = rx[v, q, pl.ds(pl.multiple_of(2 * run * pair, 16), 2 * run), :].astype(jnp.float32)
+                for t in range(2):
+                    start = pl.multiple_of((2 * NX * pair + NX * t + q) * run, 8)
+                    gbuf[v, pl.ds(start, run), :] = rows[run * t : run * (t + 1)]
+
+        @pl.loop(0, NY)
+        def _(t):
             for r in range(rows_y // 16):
                 two = [gbuf[v, pl.ds((16 * r + 8 * q) * NY + t, 8, stride=NY), :] for q in range(2)]
-                qy[t, 16 * r : 16 * (r + 1), LANES * v : LANES * (v + 1)] = jnp.concatenate(
-                    two, axis=0
-                ).astype(jnp.bfloat16)
-
-    fb[core, y] = qy[y]
-    copies = []
-    for d in range(1, NY):
-        t, device = at_y(d)
-        copies.append(send(qy.at[t], fb.at[core, y], device))
-    mate_copies = [send(fb.at[core, y], fb.at[core, y], mate)]
-    for d, copy in enumerate(copies, 1):
-        copy.wait_recv()
-        source = lax.rem(y - d + NY, NY)
-        mate_copies.append(send(fb.at[core, source], fb.at[core, source], mate))
-    for copy in mate_copies:
+                qy[v, t, 16 * r : 16 * (r + 1), :] = jnp.concatenate(two, axis=0).astype(jnp.bfloat16)
+
+        fb[core, v, y] = qy[v, y]
+        copies = []
+        for d in range(1, NY):
+            t, device = at_y(d)
+            copies.append(send(qy.at[v, t], fb.at[core, v, y], device))
+        return copies
+
+    def to_mate(v, copies):
+        mates = []
+        for d in range(NY):
+            if d:
+                copies[d - 1].wait_recv()
+            source = lax.rem(y - d + NY, NY)
+            mates.append(send(fb.at[core, v, source], fb.at[core, v, source], mate))
+        return mates
+
+    chunks = LH // LANES
+    in_z = [to_z(v) for v in range(chunks)]
+    in_x, in_y, in_mate = [], [], []
+    for step in range(chunks + 2):
+        if step < chunks:
+            for copy in in_z[step]:
+                copy.wait_recv()
+            in_x.append(to_x(step))
+        if 0 <= step - 1 < chunks:
+            for copy in in_x[step - 1]:
+                copy.wait_recv()
+            in_y.append(to_y(step - 1))
+        if 0 <= step - 2 < chunks:
+            in_mate += to_mate(step - 2, in_y[step - 2])
+    for copy in in_mate:
         copy.wait_recv()
 
     cur[...] = wt[...].astype(jnp.bfloat16)
     prop[...] = wt[...]
     for degree in range(1, 5):
-        field = jnp.concatenate([fb[0].reshape(M, LH), fb[1].reshape(M, LH)], axis=1)
+        field = jnp.concatenate(
+            [fb[q, v].reshape(M, LANES) for q in range(2) for v in range(chunks)], axis=1
+        )
         term = jnp.dot(field, cur[...], preferred_element_type=jnp.float32)
         if degree > 1:
             term = term / degree
@@ -302,12 +322,13 @@
             cur[...] = term.astype(jnp.bfloat16)
 
     rows_c = M // (2 * NX)
+    low[...] = prop[...].astype(jnp.bfloat16)
     copies = []
     own_slot = lax.rem(w, 2) * NX + x
     for dx, dc, dp, tc, device in finals:
-        start = pl.multiple_of(rows_c * tc, 8)
-        copies.append(send(prop.at[pl.ds(start, rows_c)], cand.at[own_slot, core], device))
-    cand[own_slot, core] = prop[pl.ds(pl.multiple_of(rows_c * c, 8), rows_c), :]
+        start = pl.multiple_of(rows_c * tc, 16)
+        copies.append(send(low.at[pl.ds(start, rows_c)], cand.at[own_slot, core], device))
+    cand[own_slot, core] = low[pl.ds(pl.multiple_of(rows_c * c, 16), rows_c), :]
 
     first = lax.div(w, 2) * (2 * NX)
     sums = counts[first]
@@ -322,8 +343,8 @@
         copy.wait_recv()
     lane = lax.broadcasted_iota(jnp.int32, (rows_c, LANES), 1)
     for j in range(NX):
-        up = cand[source[j], 0]
-        down = pltpu.roll(cand[source[j], 1], HALF_E - SHIFT, 1)
+        up = cand[source[j], 0].astype(jnp.float32)
+        down = pltpu.roll(cand[source[j], 1].astype(jnp.float32), HALF_E - SHIFT, 1)
         out[j, :, 0:LANES] = jnp.where(lane < HALF_E, up, down)
         out[j, :, LANES : 2 * HALF_E] = down[:, : 2 * HALF_E - LANES]
 
@@ -341,6 +362,7 @@
     chol = chol_vectors.transpose(1, 0, 2)
     f32, bf16 = jnp.float32, jnp.bfloat16
     rows_y, rows_c, block = M // NY, M // (2 * NX), WALKERS // NZ
+    chunks = LH // LANES
     vmem = pltpu.VMEM
     scratch = dict(
         wbuf=vmem((2 * HALF_E, M), f32),
@@ -354,26 +376,24 @@
         s2=vmem((NZ, KW * NY, LANES), bf16),
         mx=vmem((NX, NZ, KW * NY, LANES), bf16),
         mbig=vmem((NZ, block, KW * LANES), bf16),
-        fsend=vmem((WALKERS, GROUP), f32),
-        fown=vmem((WALKERS, GROUP), f32),
-        frecv=vmem((WALKERS, GROUP), f32),
-        fz=vmem((NZ, block, GROUP), f32),
-        fr=vmem((NZ, block, GROUP), f32),
-        fy=vmem((block, GROUP), f32),
-        fyr=vmem((NY, block, GROUP), f32),
+        fz=vmem((2, NZ, block, GROUP), bf16),
+        fr=vmem((2, NZ, block, GROUP), bf16),
+        fy=vmem((block, GROUP), bf16),
+        fyr=vmem((NY, block, GROUP), bf16),
         drawbuf=vmem((WALKERS, GROUP), f32),
         sg=vmem((2 * NX, NZ, block, GROUP), bf16),
         cr=vmem((2 * NX, XI, GROUP, LH), bf16),
-        pz=vmem((NZ, XI * block, LH), bf16),
-        rz=vmem((NZ, XI * block, LH), bf16),
-        qx=vmem((NX, NZ * XI * NY, LH), bf16),
-        rx=vmem((NX, NZ * XI * NY, LH), bf16),
-        gbuf=vmem((LH // LANES, NZ * NX * XI * NY, LANES), f32),
-        qy=vmem((NY, rows_y, LH), bf16),
-        fb=vmem((2, NY, rows_y, LH), bf16),
+        pz=vmem((chunks, NZ, XI * block, LANES), bf16),
+        rz=vmem((chunks, NZ, XI * block, LANES), bf16),
+        qx=vmem((chunks, NX, NZ * XI * NY, LANES), bf16),
+        rx=vmem((chunks, NX, NZ * XI * NY, LANES), bf16),
+        gbuf=vmem((chunks, NZ * NX * XI * NY, LANES), f32),
+        qy=vmem((chunks, NY, rows_y, LANES), bf16),
+        fb=vmem((2, chunks, NY, rows_y, LANES), bf16),
         cur=vmem((M, LANES), bf16),
         prop=vmem((M, LANES), f32),
-        cand=vmem((2 * NX, 2, rows_c, LANES), f32),
+        low=vmem((M, LANES), bf16),
+        cand=vmem((2 * NX, 2, rows_c, LANES), bf16),
         ssem=pltpu.SemaphoreType.DMA((COPIES,)),
         rsem=pltpu.SemaphoreType.DMA((COPIES,)),
         lsem=pltpu.SemaphoreType.DMA((4,)),
@@ -388,7 +408,7 @@
         out_specs=in_vmem,
         scratch_shapes=list(scratch.values()),
         compiler_params=pltpu.CompilerParams(
-            collective_id=0, has_side_effects=True, vmem_limit_bytes=48 * 2**20
+            collective_id=0, has_side_effects=True, vmem_limit_bytes=63 * 2**20
         ),
     )(walkers, inverse, half, chol, field_draw, counts)
     return result.transpose(0, 2, 1)

time: 141 us -> 111 us (0.79)
  Pallas kernels: 133 us -> 107 us
  local copies, waits for them, and re-layouts: 7.78 us -> 2.79 us
    pallas_call x1, Pallas kernels: 133 us -> 107 us  [local(): pl.pallas_call(kernel, out_shape=jax.ShapeDtypeStruct((NX, rows_c, 2 * HA...]
    unnamed x13 -> x3, local copies, waits for them, and re-layouts: 7.76 us -> 2.77 us
where the time goes in v2:
time: 111 us
  Pallas kernels  107 us (96%)
  local copies, waits for them, and re-layouts  2.79 us (3%)
    pallas_call x1, Pallas kernels, local(): pl.pallas_call(kernel, out_shape=jax.ShapeDtypeStruct((NX, rows_c, 2 * HA...  107 us
    unnamed x3, local copies, waits for them, and re-layouts  2.77 us

profile of v2, /device:TPU:1, one launch (start us, length us, event | category | flops | bytes accessed | tf_op | source)
XLA Modules:
  0.0 110.6 jit_solution(7621769321175009058)
XLA Ops:
  0.0 0.0 copy-start
  0.0 1.0 copy-done
  1.0 0.7 fusion.1.inverse
  1.8 107.1 %shard_map.64 = f32[4,96,200]{2,1,0:T(8,128)} custom-call(f32[4,200,768]{2,1,0:T(8,128)} %walkers.1, f32[128,128]{1,0:T(8,128)} %fusion.1.inverse, bf16[12,200,128]{2,1,0:T(8,128)(2,1)} %bitcast.10, bf16[12,128,768]{2,1,0:T(8,128)(2,1)} %bitcast.8, f32[256,128]{1,0:T(8,128)} %draw.1, s32[256]{0:T(256)} %counts.1), custom_call_target="tpu_custom_call" | custom-call | tf_op jit(solution)/shard_map/pallas_call | solution.py:404
  108.8 1.8 %copy.11 = f32[4,200,96]{1,2,0:T(8,128)} copy(f32[4,200,96]{1,2,0:T(8,128)} %bitcast.9) | data formatting | bytes 614400
  (2 shorter events, 0.0 us)
Async XLA Ops:
  0.0 1.0 copy-start

commit v3 on v2

v3 whole, which is shorter than its diff:
```python
import jax
import jax.numpy as jnp
from jax import lax
from jax.experimental import pallas as pl
from jax.experimental.pallas import tpu as pltpu
from jax.sharding import PartitionSpec as P

root_step = 0.1

NX, NY, NZ = 4, 8, 8
LANES = 128
HALF_E = 100
SHIFT = LANES - HALF_E
M = 768
LH = M // 2
KW = M // (NY * NZ)
XI = KW // NX
WALKERS = NX * NY * NZ
GROUP = 128
COPIES = 256
FAR_FIRST = (4, 3, 5, 2, 6, 1, 7)
NEAR_FIRST = (1, 7, 2, 6, 3, 5, 4)
CHOL_FIRST = ((1, 0), (3, 0), (0, 1), (1, 1), (3, 1))
CHOL_LAST = ((2, 0), (2, 1))
MESH = pl.DeviceIdType.MESH


def kernel(
    walkers, inverse, half, chol, draw, counts, out,
    wbuf, ibuf, ipad, wt, hbuf, hs, hsend, m1, s1, s1f, s2, mx, mbig, swap, psend, precv, fz, fr, fy, fyr,
    drawbuf, owndraw, sg, cr, pz, rz, qx, rx, gbuf, qy, rb, fb, cur, prop, low, cand, ssem, rsem, lsem,
):
    c = lax.axis_index("chol")
    w = lax.axis_index("walk")
    x = lax.div(c, 2)
    core = lax.rem(c, 2)
    y = lax.div(w, NZ)
    z = lax.rem(w, NZ)
    other = 1 - core
    partner_w = w + 1 - 2 * lax.rem(w, 2)

    p = z + core * (y - z)
    q = y + core * (z - y)
    step_p, step_q = 1 + (NZ - 1) * core, NZ - (NZ - 1) * core

    def at_p(d):
        t = lax.rem(p + d, NZ)
        return t, (c, t * step_p + q * step_q)

    def at_q(d):
        t = lax.rem(q + d, NY)
        return t, (c, p * step_p + t * step_q)

    def at_x(d):
        t = lax.rem(x + d, NX)
        return t, (t * 2 + core, w)

    mate = (x * 2 + other, w)

    barrier = pltpu.get_barrier_semaphore()
    greeted = 0
    peers = [at_q(d)[1] for d in range(1, NY)] + [at_p(d)[1] for d in range(1, NZ)]
    finals = []
    for dx in range(NX):
        for dc in range(2):
            tx = lax.rem(x + dx, NX)
            tc = tx * 2 + (core if dc == 0 else other)
            for dp in range(2):
                if dx or dc or dp:
                    finals.append((dx, dc, dp, tc, (tc, partner_w if dp else w)))
                    if dx or dc:
                        peers.append((tc, partner_w if dp else w))
    for peer in peers:
        pl.semaphore_signal(barrier, inc=1, device_id=peer, device_id_type=MESH)
        greeted += 1

    started = []

    def send(src, dst, device):
        i = len(started)
        copy = pltpu.make_async_remote_copy(
            src_ref=src, dst_ref=dst, send_sem=ssem.at[i], recv_sem=rsem.at[i],
            device_id=device, device_id_type=MESH,
        )
        copy.start()
        started.append(copy)
        return copy

    load_w = pltpu.make_async_copy(walkers.at[x], wbuf, lsem.at[0])
    load_h = pltpu.make_async_copy(half, hbuf, lsem.at[1])
    load_d = pltpu.make_async_copy(draw, drawbuf, lsem.at[2])
    load_c = pltpu.make_async_copy(
        chol.at[pl.ds(XI * x, XI), :, pl.ds(pl.multiple_of(LH * core, LANES), LH)], cr.at[c], lsem.at[3]
    )
    load_i = pltpu.make_async_copy(inverse.at[x], ibuf, lsem.at[4])
    load_i.start()
    load_w.start()
    load_h.start()
    load_d.start()
    load_c.start()

    load_w.wait()
    electron = lax.broadcasted_iota(jnp.int32, (LANES, M), 0)
    up = jnp.where(electron < HALF_E, wbuf[0:LANES, :], 0.0)
    down = jnp.where(electron >= SHIFT, wbuf[2 * HALF_E - LANES : 2 * HALF_E, :], 0.0)
    wt[...] = jnp.where(core == 0, up, down).T
    wide = wt[...]
    wide_hi = wide.astype(jnp.bfloat16)
    wide_lo = (wide - wide_hi.astype(jnp.float32)).astype(jnp.bfloat16)
    load_i.wait()
    ipad[...] = jnp.zeros_like(ipad)
    ipad[0:HALF_E, 0:HALF_E] = ibuf[pl.ds(core, HALF_E, stride=2), :]
    inv = ipad[...]
    inv = jnp.where(core == 0, inv, pltpu.roll(pltpu.roll(inv, SHIFT, 0), SHIFT, 1))
    inv_hi = inv.astype(jnp.bfloat16)
    inv_lo = (inv - inv_hi.astype(jnp.float32)).astype(jnp.bfloat16)
    mixed = lax.dot_general(
        jnp.concatenate([wide_hi, wide_lo, wide_hi, wide_lo], axis=1),
        jnp.concatenate([inv_hi, inv_hi, inv_lo, inv_lo], axis=1),
        (((1,), (1,)), ((), ())),
        preferred_element_type=jnp.float32,
    )
    rows_y = M // NY

    @pl.when(core == 0)
    def _():
        m1[...] = mixed.astype(jnp.bfloat16).reshape(NY, rows_y, LANES)

    @pl.when(core == 1)
    def _():
        s1f[...] = mixed

        @pl.loop(0, NZ)
        def _(t):
            for r in range(KW // 2):
                pair = [s1f[pl.ds(KW * t + 2 * r + h, NY, stride=rows_y), :] for h in range(2)]
                m1[t, 16 * r : 16 * (r + 1)] = jnp.concatenate(pair, axis=0).astype(jnp.bfloat16)

    s1[q] = m1[q]

    pl.semaphore_wait(barrier, greeted)

    copies = []
    for d in FAR_FIRST:
        t, device = at_q(d)
        copies.append(send(m1.at[t], s1.at[q], device))

    chol_copies = []

    def send_chol(pieces):
        for dx, dc in pieces:
            tx = lax.rem(x + dx, NX)
            tcore = core if dc == 0 else other
            columns = pl.ds(pl.multiple_of(LH * tcore, LANES), LH)
            chol_copies.append(
                send(chol.at[pl.ds(XI * tx, XI), :, columns], cr.at[c], (tx * 2 + tcore, w))
            )

    send_chol(CHOL_FIRST)

    load_h.wait()
    for k in range(KW):
        rows = hbuf[k].astype(jnp.float32)
        first = rows[0:LANES]
        second = rows[2 * HALF_E - LANES : 2 * HALF_E]
        hs[core, LANES * k : LANES * (k + 1)] = jnp.where(core == 0, first, second).astype(jnp.bfloat16)
        hsend[LANES * k : LANES * (k + 1)] = jnp.where(core == 0, second, first).astype(jnp.bfloat16)
    half_copy = send(hsend, hs.at[core], mate)

    row = lax.broadcasted_iota(jnp.int32, (WALKERS, WALKERS), 0)
    column = lax.broadcasted_iota(jnp.int32, (WALKERS, WALKERS), 1)
    target = (row & 7) * (WALKERS // NZ) + (row & 24) + (row >> 5)
    swap[...] = jnp.where(column == target, 1.0, 0.0).astype(jnp.bfloat16)

    load_d.wait()

    @pl.when(core == 0)
    def _():
        for g in range(NX):
            owndraw[8 * g : 8 * (g + 1)] = drawbuf[pl.ds(NX * z + g, NY, stride=NX * NZ), :]

    @pl.when(core == 1)
    def _():
        for g in range(NX):
            owndraw[8 * g : 8 * (g + 1)] = drawbuf[pl.ds(NX * NZ * y + g, NZ, stride=NX), :]

    for copy in copies:
        copy.wait_recv()

    for t in range(NY):
        s1f[rows_y * t : rows_y * (t + 1)] = s1[t].astype(jnp.float32)

    @pl.loop(0, NZ)
    def _(t):
        for r in range(KW // 2):
            pair = []
            for h in range(2):
                first = t * (KW - (KW - 1) * core) + (2 * r + h) * (1 + (NY - 1) * core)
                pair.append(s1f[pl.ds(first, NY, stride=rows_y), :])
            s2[t, 16 * r : 16 * (r + 1)] = jnp.concatenate(pair, axis=0).astype(jnp.bfloat16)

    mx[x, p] = s2[p]
    copies = []
    for d in FAR_FIRST:
        t, device = at_p(d)
        copies.append(send(s2.at[t], mx.at[x, p], device))

    x_copies = []
    for d in (0,) + NEAR_FIRST:
        if d:
            copies[FAR_FIRST.index(d)].wait_recv()
        source = lax.rem(p - d + NZ, NZ)
        for e in (2, 1, 3):
            x_copies.append(send(mx.at[x, source], mx.at[x, source], at_x(e)[1]))
    for copy in x_copies:
        copy.wait_recv()
    send_chol(CHOL_LAST)

    @pl.loop(0, NZ)
    def _(t):
        for r in range(KW // 2):
            blocks = [mx[g, t, 16 * r : 16 * (r + 1)].astype(jnp.float32) for g in range(NX)]
            for h in range(2):
                rows = jnp.concatenate([b[8 * h : 8 * (h + 1)] for b in blocks], axis=0)
                k = 2 * r + h
                mbig[t, :, LANES * k : LANES * (k + 1)] = rows.astype(jnp.bfloat16)

    half_copy.wait_recv()
    vectors = jnp.concatenate([hs[0], hs[1]], axis=1)
    bias = jnp.dot(
        mbig[...].reshape(WALKERS, KW * LANES), vectors, preferred_element_type=jnp.float32
    )
    low_part, high_part = bias[:, :GROUP], bias[:, GROUP:]
    theirs = jnp.where(core == 0, high_part, low_part).astype(jnp.bfloat16)
    psend[...] = jnp.dot(swap[...], theirs, preferred_element_type=jnp.float32).astype(jnp.bfloat16)
    spin_copy = send(psend, precv, mate)
    ours = jnp.where(core == 0, low_part, high_part)
    spin_copy.wait_recv()
    both = (ours + precv[...].astype(jnp.float32)).astype(jnp.bfloat16)
    fz[...] = both.reshape(NZ, WALKERS // NZ, GROUP)

    fr[p] = fz[p]
    copies = []
    for d in FAR_FIRST:
        t, device = at_p(d)
        copies.append(send(fz.at[t], fr.at[p], device))
    for copy in copies:
        copy.wait_recv()
    fy[...] = jnp.sum(fr[...].astype(jnp.float32), axis=0).astype(jnp.bfloat16)
    fyr[q] = fy[...]
    copies = []
    for d in FAR_FIRST:
        t, device = at_q(d)
        copies.append(send(fy, fyr.at[q], device))
    for copy in copies:
        copy.wait_recv()
    total = jnp.sum(fyr[...].astype(jnp.float32), axis=0)
    sg[c, p] = (owndraw[...] + root_step * total).astype(jnp.bfloat16)

    copies = []
    for d in FAR_FIRST:
        t, device = at_p(d)
        copies.append(send(sg.at[c, p], sg.at[c, p], device))
    x_copies = []
    for d in (0,) + NEAR_FIRST:
        if d:
            copies[FAR_FIRST.index(d)].wait_recv()
        source = lax.rem(p - d + NZ, NZ)
        for e in (2, 1, 3):
            x_copies.append((e, send(sg.at[c, source], sg.at[c, source], at_x(e)[1])))
    mate_copies = [send(sg.at[c], sg.at[c], mate)]
    for e in (1, 3, 2):
        for offset, copy in x_copies:
            if offset == e:
                copy.wait_recv()
        source = lax.rem(x - e + NX, NX) * 2 + core
        mate_copies.append(send(sg.at[source], sg.at[source], mate))
    for copy in mate_copies:
        copy.wait_recv()
    load_c.wait()
    for copy in chol_copies:
        copy.wait_recv()

    shifted = jnp.concatenate([sg[2 * g + core].reshape(WALKERS, GROUP) for g in range(NX)], axis=1)
    swapped = jnp.concatenate([sg[2 * g + other].reshape(WALKERS, GROUP) for g in range(NX)], axis=1)
    swapped = jnp.dot(swap[...], swapped, preferred_element_type=jnp.float32).astype(jnp.bfloat16)
    shifted = jnp.concatenate([shifted, swapped], axis=1)
    block = WALKERS // NZ
    run = XI * NY

    def to_p(v):
        lanes = slice(LANES * v, LANES * (v + 1))
        columns = jnp.concatenate(
            [
                jnp.concatenate([cr[2 * g + h, i, :, lanes] for i in range(XI)], axis=1)
                for h in (core, other)
                for g in range(NX)
            ],
            axis=0,
        )
        product = jnp.dot(shifted, columns, preferred_element_type=jnp.float32)
        product = (root_step * product).astype(jnp.bfloat16)
        for i in range(XI):
            part = product[:, LANES * i : LANES * (i + 1)]
            pz[v, :, block * i : block * (i + 1), :] = part.reshape(NZ, block, LANES)
        rz[v, p] = pz[v, p]
        copies = []
        for d in FAR_FIRST:
            t, device = at_p(d)
            copies.append(send(pz.at[v, t], rz.at[v, p], device))
        return copies

    def to_x(v):
        @pl.loop(0, NZ // 2)
        def _(pair):
            tiles = []
            for t in range(2):
                for i in range(XI):
                    tiles.append(rz[v, 2 * pair + t, block * i : block * (i + 1), :].astype(jnp.float32))
            for r in range(XI):
                for g in range(NX):
                    two = [tiles[2 * r + h][8 * g : 8 * (g + 1)] for h in range(2)]
                    start = pl.multiple_of(2 * run * pair + 16 * r, 16)
                    qx[v, g, pl.ds(start, 16), :] = jnp.concatenate(two, axis=0).astype(jnp.bfloat16)

        rx[v, x] = qx[v, x]
        copies = []
        for d in range(1, NX):
            t, device = at_x(d)
            copies.append(send(qx.at[v, t], rx.at[v, x], device))
        return copies

    def strided(v, put):
        @pl.loop(0, NY)
        def _(t):
            for r in range(rows_y // 16):
                two = [gbuf[v, pl.ds((16 * r + 8 * h) * NY + t, 8, stride=NY), :] for h in range(2)]
                put(t, 16 * r, jnp.concatenate(two, axis=0).astype(jnp.bfloat16))

    def to_q(v):
        @pl.loop(0, NZ // 2)
        def _(pair):
            for g in range(NX):
                rows = rx[v, g, pl.ds(pl.multiple_of(2 * run * pair, 16), 2 * run), :].astype(jnp.float32)
                for t in range(2):
                    for i in range(XI):
                        at = (2 * pair + t) * (KW - (KW - 1) * core) + (XI * g + i) * (1 + (NY - 1) * core)
                        start = pl.multiple_of(NY * at, 8)
                        gbuf[v, pl.ds(start, 8), :] = rows[run * t + 8 * i : run * t + 8 * (i + 1)]

        def put(t, r, rows):
            qy[v, t, r : r + 16, :] = rows

        strided(v, put)
        rb[v, q] = qy[v, q]
        copies = []
        for d in FAR_FIRST:
            t, device = at_q(d)
            copies.append(send(qy.at[v, t], rb.at[v, q], device))
        return copies

    def to_mate(v):
        @pl.when(core == 0)
        def _():
            fb[0, v] = rb[v]

        @pl.when(core == 1)
        def _():
            gbuf[v] = rb[v].astype(jnp.float32).reshape(M, LANES)

            def put(t, r, rows):
                fb[1, v, t, r : r + 16, :] = rows

            strided(v, put)

        return send(fb.at[core, v], fb.at[core, v], mate)

    chunks = LH // LANES
    in_p = [to_p(v) for v in range(chunks)]
    in_x, in_q, in_mate = [], [], []
    for step in range(chunks + 2):
        if step < chunks:
            for copy in in_p[step]:
                copy.wait_recv()
            in_x.append(to_x(step))
        if 0 <= step - 1 < chunks:
            for copy in in_x[step - 1]:
                copy.wait_recv()
            in_q.append(to_q(step - 1))
        if 0 <= step - 2 < chunks:
            for copy in in_q[step - 2]:
                copy.wait_recv()
            in_mate.append(to_mate(step - 2))
    for copy in in_mate:
        copy.wait_recv()

    cur[...] = wt[...].astype(jnp.bfloat16)
    prop[...] = wt[...]
    for degree in range(1, 5):
        field = jnp.concatenate(
            [fb[q, v].reshape(M, LANES) for q in range(2) for v in range(chunks)], axis=1
        )
        term = jnp.dot(field, cur[...], preferred_element_type=jnp.float32)
        if degree > 1:
            term = term / degree
        prop[...] += term
        if degree < 4:
            cur[...] = term.astype(jnp.bfloat16)

    rows_c = M // (2 * NX)
    low[...] = prop[...].astype(jnp.bfloat16)
    copies = []
    own_slot = lax.rem(w, 2) * NX + x
    for dx, dc, dp, tc, device in finals:
        start = pl.multiple_of(rows_c * tc, 16)
        copies.append(send(low.at[pl.ds(start, rows_c)], cand.at[own_slot, core], device))
    cand[own_slot, core] = low[pl.ds(pl.multiple_of(rows_c * c, 16), rows_c), :]

    first = lax.div(w, 2) * (2 * NX)
    sums = counts[first]
    source = [jnp.int32(0)] * NX
    for i in range(2 * NX):
        if i:
            sums = sums + counts[first + i]
        for j in range(NX):
            source[j] = source[j] + jnp.where(sums <= lax.rem(w, 2) * NX + j, 1, 0)
    source = [jnp.minimum(s, 2 * NX - 1) for s in source]
    for copy in copies:
        copy.wait_recv()
    lane = lax.broadcasted_iota(jnp.int32, (rows_c, LANES), 1)
    for j in range(NX):
        up = cand[source[j], 0].astype(jnp.float32)
        down = pltpu.roll(cand[source[j], 1].astype(jnp.float32), HALF_E - SHIFT, 1)
        out[j, :, 0:LANES] = jnp.where(lane < HALF_E, up, down)
        out[j, :, LANES : 2 * HALF_E] = down[:, : 2 * HALF_E - LANES]

    for copy in started:
        copy.wait_send()


def local(walkers, inv_intersection, half_vectors, chol_vectors, field_draw, counts):
    inverse = inv_intersection.transpose(0, 2, 1, 3).reshape(NX, 2 * HALF_E, HALF_E)
    half = half_vectors.transpose(2, 1, 0)
    chol = chol_vectors.transpose(1, 0, 2)
    f32, bf16 = jnp.float32, jnp.bfloat16
    rows_y, rows_c, block = M // NY, M // (2 * NX), WALKERS // NZ
    chunks = LH // LANES
    vmem = pltpu.VMEM
    scratch = dict(
        wbuf=vmem((2 * HALF_E, M), f32),
        ibuf=vmem((2 * HALF_E, HALF_E), f32),
        ipad=vmem((LANES, LANES), f32),
        wt=vmem((M, LANES), f32),
        hbuf=vmem((KW, 2 * HALF_E, GROUP), bf16),
        hs=vmem((2, KW * LANES, GROUP), bf16),
        hsend=vmem((KW * LANES, GROUP), bf16),
        m1=vmem((NY, rows_y, LANES), bf16),
        s1=vmem((NY, rows_y, LANES), bf16),
        s1f=vmem((NY * rows_y, LANES), f32),
        s2=vmem((NZ, KW * NY, LANES), bf16),
        mx=vmem((NX, NZ, KW * NY, LANES), bf16),
        mbig=vmem((NZ, block, KW * LANES), bf16),
        swap=vmem((WALKERS, WALKERS), bf16),
        psend=vmem((WALKERS, GROUP), bf16),
        precv=vmem((WALKERS, GROUP), bf16),
        fz=vmem((NZ, block, GROUP), bf16),
        fr=vmem((NZ, block, GROUP), bf16),
        fy=vmem((block, GROUP), bf16),
        fyr=vmem((NY, block, GROUP), bf16),
        drawbuf=vmem((WALKERS, GROUP), f32),
        owndraw=vmem((block, GROUP), f32),
        sg=vmem((2 * NX, NZ, block, GROUP), bf16),
        cr=vmem((2 * NX, XI, GROUP, LH), bf16),
        pz=vmem((chunks, NZ, XI * block, LANES), bf16),
        rz=vmem((chunks, NZ, XI * block, LANES), bf16),
        qx=vmem((chunks, NX, NZ * XI * NY, LANES), bf16),
        rx=vmem((chunks, NX, NZ * XI * NY, LANES), bf16),
        gbuf=vmem((chunks, NZ * NX * XI * NY, LANES), f32),
        qy=vmem((chunks, NY, rows_y, LANES), bf16),
        rb=vmem((chunks, NY, rows_y, LANES), bf16),
        fb=vmem((2, chunks, NY, rows_y, LANES), bf16),
        cur=vmem((M, LANES), bf16),
        prop=vmem((M, LANES), f32),
        low=vmem((M, LANES), bf16),
        cand=vmem((2 * NX, 2, rows_c, LANES), bf16),
        ssem=pltpu.SemaphoreType.DMA((COPIES,)),
        rsem=pltpu.SemaphoreType.DMA((COPIES,)),
        lsem=pltpu.SemaphoreType.DMA((5,)),
    )
    hbm = pl.BlockSpec(memory_space=pltpu.HBM)
    in_vmem = pl.BlockSpec(memory_space=pltpu.VMEM)
    in_smem = pl.BlockSpec(memory_space=pltpu.SMEM)
    result = pl.pallas_call(
        kernel,
        out_shape=jax.ShapeDtypeStruct((NX, rows_c, 2 * HALF_E), f32),
        in_specs=[hbm, hbm, hbm, hbm, hbm, in_smem],
        out_specs=in_vmem,
        scratch_shapes=list(scratch.values()),
        compiler_params=pltpu.CompilerParams(
            collective_id=0, has_side_effects=True, vmem_limit_bytes=63 * 2**20
        ),
    )(walkers, inverse, half, chol, field_draw, counts)
    return result.transpose(0, 2, 1)


def solution(mesh):
    placed = (
        P("walk", None, None),
        P("walk", None, None, None),
        P("chol", None, "walk"),
        P("chol", "walk", None),
        P(None, "chol"),
        P(),
    )
    return jax.shard_map(
        local, mesh=mesh, in_specs=placed, out_specs=P("walk", None, "chol"), check_vma=False
    )
```

time: 111 us -> 98.2 us (0.88)
  Pallas kernels: 107 us -> 96.2 us
    pallas_call x1, Pallas kernels: 107 us -> 96.2 us  [local(): pl.pallas_call(kernel, out_shape=jax.ShapeDtypeStruct((NX, rows_c, 2 * HA...]
    unnamed x3 -> x1, local copies, waits for them, and re-layouts: 2.77 us -> 1.77 us
where the time goes in v3:
time: 98.2 us; the launch traced here: 98 us
  Pallas kernels  96.2 us (98%)
  local copies, waits for them, and re-layouts  1.77 us (2%)
    pallas_call x1, Pallas kernels, local(): pl.pallas_call(kernel, out_shape=jax.ShapeDtypeStruct((NX, rows_c, 2 * HA...  96.2 us

profile of v3, /device:TPU:1, one launch (start us, length us, event | category | flops | bytes accessed | tf_op | source)
XLA Modules:
  0.0 98.0 jit_solution(5338397615607390858)
XLA Ops:
  0.0 96.2 %shard_map.64 = f32[4,96,200]{2,1,0:T(8,128)} custom-call(f32[4,200,768]{2,1,0:T(8,128)} %walkers.1, f32[4,200,100]{2,1,0:T(8,128)} %bitcast.9, bf16[12,200,128]{2,1,0:T(8,128)(2,1)} %bitcast.8, bf16[12,128,768]{2,1,0:T(8,128)(2,1)} %bitcast.6, f32[256,128]{1,0:T(8,128)} %draw.1, s32[256]{0:T(256)} %counts.1), custom_call_target="tpu_custom_call" | custom-call | tf_op jit(solution)/shard_map/pallas_call | solution.py:493
  96.2 1.8 %copy.8 = f32[4,200,96]{1,2,0:T(8,128)} copy(f32[4,200,96]{1,2,0:T(8,128)} %bitcast.7) | data formatting | bytes 614400

commit v4 on v3

--- a/solution.py
+++ b/solution.py
@@ -20,15 +20,20 @@
 COPIES = 256
 FAR_FIRST = (4, 3, 5, 2, 6, 1, 7)
 NEAR_FIRST = (1, 7, 2, 6, 3, 5, 4)
-CHOL_FIRST = ((1, 0), (3, 0), (0, 1), (1, 1), (3, 1))
-CHOL_LAST = ((2, 0), (2, 1))
+NEAR = ((1, 0), (3, 0), (1, 1), (3, 1))
+FAR = ((2, 0), (2, 1))
+MATE = tuple((0, 1, v) for v in range(3))
+NEARS = [tuple((dx, dc, v) for dx, dc in NEAR) for v in range(3)]
+FARS = [tuple((dx, dc, v) for dx, dc in FAR) for v in range(3)]
+CHOL_PLAN = (MATE + NEARS[0] + NEARS[1], FARS[0] + FARS[1], NEARS[2], FARS[2], ())
+BIAS_PARTS = 2
 MESH = pl.DeviceIdType.MESH
 
 
 def kernel(
     walkers, inverse, half, chol, draw, counts, out,
-    wbuf, ibuf, ipad, wt, hbuf, hs, hsend, m1, s1, s1f, s2, mx, mbig, swap, psend, precv, fz, fr, fy, fyr,
-    drawbuf, owndraw, sg, cr, pz, rz, qx, rx, gbuf, qy, rb, fb, cur, prop, low, cand, ssem, rsem, lsem,
+    wbuf, ibuf, ipad, wt, hbuf, hs, hsend, m1, s1, s1f, s2, mx, mbig, biasbuf, swap, psend, precv, fz, fr, fy, fyr,
+    drawbuf, owndraw, sg, cbuf, cr, pz, rz, qx, rx, gbuf, qy, rb, fb, cur, prop, low, cand, ssem, rsem, lsem,
 ):
     c = lax.axis_index("chol")
     w = lax.axis_index("walk")
@@ -86,18 +91,34 @@
         started.append(copy)
         return copy
 
+    drained = []
+
+    def drain(but=()):
+        for copy in started:
+            if not any(copy is kept for kept in drained) and not any(copy is kept for kept in but):
+                copy.wait_send()
+                drained.append(copy)
+
     load_w = pltpu.make_async_copy(walkers.at[x], wbuf, lsem.at[0])
     load_h = pltpu.make_async_copy(half, hbuf, lsem.at[1])
     load_d = pltpu.make_async_copy(draw, drawbuf, lsem.at[2])
-    load_c = pltpu.make_async_copy(
-        chol.at[pl.ds(XI * x, XI), :, pl.ds(pl.multiple_of(LH * core, LANES), LH)], cr.at[c], lsem.at[3]
-    )
-    load_i = pltpu.make_async_copy(inverse.at[x], ibuf, lsem.at[4])
+    load_c = [
+        pltpu.make_async_copy(
+            chol.at[pl.ds(XI * x, XI), :, pl.ds(pl.multiple_of(LH * core + LANES * v, LANES), LANES)],
+            cr.at[v, c],
+            lsem.at[3 + v],
+        )
+        for v in range(LH // LANES)
+    ]
+    load_i = pltpu.make_async_copy(inverse.at[x], ibuf, lsem.at[6])
     load_i.start()
     load_w.start()
     load_h.start()
     load_d.start()
-    load_c.start()
+    for copy in load_c:
+        copy.start()
+    load_all = pltpu.make_async_copy(chol, cbuf, lsem.at[7])
+    load_all.start()
 
     load_w.wait()
     electron = lax.broadcasted_iota(jnp.int32, (LANES, M), 0)
@@ -148,15 +169,15 @@
     chol_copies = []
 
     def send_chol(pieces):
-        for dx, dc in pieces:
+        for dx, dc, v in pieces:
             tx = lax.rem(x + dx, NX)
             tcore = core if dc == 0 else other
-            columns = pl.ds(pl.multiple_of(LH * tcore, LANES), LH)
-            chol_copies.append(
-                send(chol.at[pl.ds(XI * tx, XI), :, columns], cr.at[c], (tx * 2 + tcore, w))
-            )
-
-    send_chol(CHOL_FIRST)
+            columns = pl.ds(pl.multiple_of(LH * tcore + LANES * v, LANES), LANES)
+            copy = send(cbuf.at[pl.ds(XI * tx, XI), :, columns], cr.at[v, c], (tx * 2 + tcore, w))
+            chol_copies.append((v, copy))
+
+    load_all.wait()
+    send_chol(CHOL_PLAN[0])
 
     load_h.wait()
     for k in range(KW):
@@ -211,25 +232,38 @@
             copies[FAR_FIRST.index(d)].wait_recv()
         source = lax.rem(p - d + NZ, NZ)
         for e in (2, 1, 3):
-            x_copies.append(send(mx.at[x, source], mx.at[x, source], at_x(e)[1]))
-    for copy in x_copies:
-        copy.wait_recv()
-    send_chol(CHOL_LAST)
-
-    @pl.loop(0, NZ)
-    def _(t):
-        for r in range(KW // 2):
-            blocks = [mx[g, t, 16 * r : 16 * (r + 1)].astype(jnp.float32) for g in range(NX)]
-            for h in range(2):
-                rows = jnp.concatenate([b[8 * h : 8 * (h + 1)] for b in blocks], axis=0)
-                k = 2 * r + h
-                mbig[t, :, LANES * k : LANES * (k + 1)] = rows.astype(jnp.bfloat16)
-
+            x_copies.append((d, send(mx.at[x, source], mx.at[x, source], at_x(e)[1])))
     half_copy.wait_recv()
-    vectors = jnp.concatenate([hs[0], hs[1]], axis=1)
-    bias = jnp.dot(
-        mbig[...].reshape(WALKERS, KW * LANES), vectors, preferred_element_type=jnp.float32
-    )
+
+    order = (0,) + NEAR_FIRST
+    size = NZ // BIAS_PARTS
+    for n in range(BIAS_PARTS):
+        group = order[size * n : size * (n + 1)]
+        for d in group:
+            for offset, copy in x_copies:
+                if offset == d:
+                    copy.wait_recv()
+        for j, d in enumerate(group):
+            t = lax.rem(p - d + NZ, NZ)
+            for r in range(KW // 2):
+                blocks = [mx[g, t, 16 * r : 16 * (r + 1)].astype(jnp.float32) for g in range(NX)]
+                for h in range(2):
+                    rows = jnp.concatenate([b[8 * h : 8 * (h + 1)] for b in blocks], axis=0)
+                    k = 2 * r + h
+                    mbig[size * n + j, :, LANES * k : LANES * (k + 1)] = rows.astype(jnp.bfloat16)
+        vectors = jnp.concatenate([hs[0], hs[1]], axis=1)
+        part = jnp.dot(
+            mbig[size * n : size * (n + 1)].reshape(WALKERS // BIAS_PARTS, KW * LANES),
+            vectors,
+            preferred_element_type=jnp.float32,
+        )
+        for j, d in enumerate(group):
+            t = lax.rem(p - d + NZ, NZ)
+            rows = WALKERS // NZ
+            biasbuf[t] = part[rows * j : rows * (j + 1)]
+    send_chol(CHOL_PLAN[1])
+    bias = biasbuf[...].reshape(WALKERS, 2 * GROUP)
+
     low_part, high_part = bias[:, :GROUP], bias[:, GROUP:]
     theirs = jnp.where(core == 0, high_part, low_part).astype(jnp.bfloat16)
     psend[...] = jnp.dot(swap[...], theirs, preferred_element_type=jnp.float32).astype(jnp.bfloat16)
@@ -244,6 +278,7 @@
     for d in FAR_FIRST:
         t, device = at_p(d)
         copies.append(send(fz.at[t], fr.at[p], device))
+    send_chol(CHOL_PLAN[2])
     for copy in copies:
         copy.wait_recv()
     fy[...] = jnp.sum(fr[...].astype(jnp.float32), axis=0).astype(jnp.bfloat16)
@@ -252,6 +287,7 @@
     for d in FAR_FIRST:
         t, device = at_q(d)
         copies.append(send(fy, fyr.at[q], device))
+    send_chol(CHOL_PLAN[3])
     for copy in copies:
         copy.wait_recv()
     total = jnp.sum(fyr[...].astype(jnp.float32), axis=0)
@@ -261,6 +297,7 @@
     for d in FAR_FIRST:
         t, device = at_p(d)
         copies.append(send(sg.at[c, p], sg.at[c, p], device))
+    send_chol(CHOL_PLAN[4])
     x_copies = []
     for d in (0,) + NEAR_FIRST:
         if d:
@@ -277,10 +314,6 @@
         mate_copies.append(send(sg.at[source], sg.at[source], mate))
     for copy in mate_copies:
         copy.wait_recv()
-    load_c.wait()
-    for copy in chol_copies:
-        copy.wait_recv()
-
     shifted = jnp.concatenate([sg[2 * g + core].reshape(WALKERS, GROUP) for g in range(NX)], axis=1)
     swapped = jnp.concatenate([sg[2 * g + other].reshape(WALKERS, GROUP) for g in range(NX)], axis=1)
     swapped = jnp.dot(swap[...], swapped, preferred_element_type=jnp.float32).astype(jnp.bfloat16)
@@ -289,10 +322,13 @@
     run = XI * NY
 
     def to_p(v):
-        lanes = slice(LANES * v, LANES * (v + 1))
+        load_c[v].wait()
+        for chunk, copy in chol_copies:
+            if chunk == v:
+                copy.wait_recv()
         columns = jnp.concatenate(
             [
-                jnp.concatenate([cr[2 * g + h, i, :, lanes] for i in range(XI)], axis=1)
+                jnp.concatenate([cr[v, 2 * g + h, i] for i in range(XI)], axis=1)
                 for h in (core, other)
                 for g in range(NX)
             ],
@@ -378,19 +414,21 @@
     chunks = LH // LANES
     in_p = [to_p(v) for v in range(chunks)]
     in_x, in_q, in_mate = [], [], []
-    for step in range(chunks + 2):
-        if step < chunks:
-            for copy in in_p[step]:
-                copy.wait_recv()
-            in_x.append(to_x(step))
-        if 0 <= step - 1 < chunks:
-            for copy in in_x[step - 1]:
-                copy.wait_recv()
-            in_q.append(to_q(step - 1))
-        if 0 <= step - 2 < chunks:
-            for copy in in_q[step - 2]:
-                copy.wait_recv()
-            in_mate.append(to_mate(step - 2))
+    drain(sum(in_p, []))
+    for v in range(chunks):
+        for copy in in_p[v]:
+            copy.wait_recv()
+        in_x.append(to_x(v))
+    for v in range(chunks):
+        for copy in in_x[v]:
+            copy.wait_recv()
+        in_q.append(to_q(v))
+    drain(sum(in_q, []))
+    for v in range(chunks):
+        for copy in in_q[v]:
+            copy.wait_recv()
+        in_mate.append(to_mate(v))
+    drain(in_mate)
     for copy in in_mate:
         copy.wait_recv()
 
@@ -411,7 +449,7 @@
     low[...] = prop[...].astype(jnp.bfloat16)
     copies = []
     own_slot = lax.rem(w, 2) * NX + x
-    for dx, dc, dp, tc, device in finals:
+    for dx, dc, dp, tc, device in sorted(finals, key=lambda f: (-f[2], abs(f[0] - 2))):
         start = pl.multiple_of(rows_c * tc, 16)
         copies.append(send(low.at[pl.ds(start, rows_c)], cand.at[own_slot, core], device))
     cand[own_slot, core] = low[pl.ds(pl.multiple_of(rows_c * c, 16), rows_c), :]
@@ -434,8 +472,7 @@
         out[j, :, 0:LANES] = jnp.where(lane < HALF_E, up, down)
         out[j, :, LANES : 2 * HALF_E] = down[:, : 2 * HALF_E - LANES]
 
-    for copy in started:
-        copy.wait_send()
+    drain()
 
 
 def local(walkers, inv_intersection, half_vectors, chol_vectors, field_draw, counts):
@@ -460,6 +497,7 @@
         s2=vmem((NZ, KW * NY, LANES), bf16),
         mx=vmem((NX, NZ, KW * NY, LANES), bf16),
         mbig=vmem((NZ, block, KW * LANES), bf16),
+        biasbuf=vmem((NZ, block, 2 * GROUP), f32),
         swap=vmem((WALKERS, WALKERS), bf16),
         psend=vmem((WALKERS, GROUP), bf16),
         precv=vmem((WALKERS, GROUP), bf16),
@@ -470,7 +508,8 @@
         drawbuf=vmem((WALKERS, GROUP), f32),
         owndraw=vmem((block, GROUP), f32),
         sg=vmem((2 * NX, NZ, block, GROUP), bf16),
-        cr=vmem((2 * NX, XI, GROUP, LH), bf16),
+        cbuf=vmem((KW, GROUP, M), bf16),
+        cr=vmem((chunks, 2 * NX, XI, GROUP, LANES), bf16),
         pz=vmem((chunks, NZ, XI * block, LANES), bf16),
         rz=vmem((chunks, NZ, XI * block, LANES), bf16),
         qx=vmem((chunks, NX, NZ * XI * NY, LANES), bf16),
@@ -485,11 +524,13 @@
         cand=vmem((2 * NX, 2, rows_c, LANES), bf16),
         ssem=pltpu.SemaphoreType.DMA((COPIES,)),
         rsem=pltpu.SemaphoreType.DMA((COPIES,)),
-        lsem=pltpu.SemaphoreType.DMA((5,)),
+        lsem=pltpu.SemaphoreType.DMA((8,)),
     )
     hbm = pl.BlockSpec(memory_space=pltpu.HBM)
     in_vmem = pl.BlockSpec(memory_space=pltpu.VMEM)
     in_smem = pl.BlockSpec(memory_space=pltpu.SMEM)
+    operands = [walkers, inverse, half, chol, field_draw, counts]
+    operands = [pltpu.with_memory_space_constraint(v, pltpu.HBM) for v in operands]
     result = pl.pallas_call(
         kernel,
         out_shape=jax.ShapeDtypeStruct((NX, rows_c, 2 * HALF_E), f32),
@@ -497,9 +538,9 @@
         out_specs=in_vmem,
         scratch_shapes=list(scratch.values()),
         compiler_params=pltpu.CompilerParams(
-            collective_id=0, has_side_effects=True, vmem_limit_bytes=63 * 2**20
+            collective_id=0, has_side_effects=True, vmem_limit_bytes=48 * 2**20
         ),
-    )(walkers, inverse, half, chol, field_draw, counts)
+    )(*operands)
     return result.transpose(0, 2, 1)
 
 

time: 98.2 us -> 95.2 us (0.969)
  Pallas kernels: 96.2 us -> 94.3 us
  local copies, waits for them, and re-layouts: 1.77 us -> 0.75 us
    pallas_call x1, Pallas kernels: 96.2 us -> 94.3 us  [local(): pl.pallas_call(kernel, out_shape=jax.ShapeDtypeStruct((NX, rows_c, 2 * HA...]
    unnamed x1, local copies, waits for them, and re-layouts: 1.77 us -> 0.75 us
where the time goes in v4:
time: 95.2 us; the launch traced here: 95 us
  Pallas kernels  94.3 us (99%)
    pallas_call x1, Pallas kernels, local(): pl.pallas_call(kernel, out_shape=jax.ShapeDtypeStruct((NX, rows_c, 2 * HA...  94.3 us

profile of v4, /device:TPU:1, one launch (start us, length us, event | category | flops | bytes accessed | tf_op | source)
XLA Modules:
  0.0 95.0 jit_solution(12166665487155117917)
XLA Ops:
  0.0 94.3 %shard_map.64 = f32[4,96,200]{2,1,0:T(8,128)S(1)} custom-call(f32[4,200,768]{2,1,0:T(8,128)} %walkers.1, f32[4,200,100]{2,1,0:T(8,128)} %bitcast.9, bf16[12,200,128]{2,1,0:T(8,128)(2,1)} %bitcast.8, bf16[12,128,768]{2,1,0:T(8,128)(2,1)} %bitcast.7, f32[256,128]{1,0:T(8,128)} %draw.1, s32[256]{0:T(256)} %counts.1), custom_call_target="tpu_custom_call" | custom-call | tf_op jit(solution)/shard_map/pallas_call | solution.py:534
  94.3 0.7 copy.8

commit v5 on v4

--- a/solution.py
+++ b/solution.py
@@ -26,7 +26,7 @@
 NEARS = [tuple((dx, dc, v) for dx, dc in NEAR) for v in range(3)]
 FARS = [tuple((dx, dc, v) for dx, dc in FAR) for v in range(3)]
 CHOL_PLAN = (MATE + NEARS[0] + NEARS[1], FARS[0] + FARS[1], NEARS[2], FARS[2], ())
-BIAS_PARTS = 2
+BIAS_PARTS = 1
 MESH = pl.DeviceIdType.MESH
 
 
@@ -361,7 +361,7 @@
 
         rx[v, x] = qx[v, x]
         copies = []
-        for d in range(1, NX):
+        for d in (2, 1, 3):
             t, device = at_x(d)
             copies.append(send(qx.at[v, t], rx.at[v, x], device))
         return copies

time: 95.2 us -> 95.5 us (level)
  no operation moved by 1% of the time
where the time goes in v5:
time: 95.5 us; the launch traced here: 95.4 us
  Pallas kernels  94.6 us (99%)
    pallas_call x1, Pallas kernels, local(): pl.pallas_call(kernel, out_shape=jax.ShapeDtypeStruct((NX, rows_c, 2 * HA...  94.6 us

profile of v5, /device:TPU:1, one launch (start us, length us, event | category | flops | bytes accessed | tf_op | source)
XLA Modules:
  0.0 95.4 jit_solution(16693098435428920613)
XLA Ops:
  0.0 94.6 %shard_map.64 = f32[4,96,200]{2,1,0:T(8,128)S(1)} custom-call(f32[4,200,768]{2,1,0:T(8,128)} %walkers.1, f32[4,200,100]{2,1,0:T(8,128)} %bitcast.9, bf16[12,200,128]{2,1,0:T(8,128)(2,1)} %bitcast.8, bf16[12,128,768]{2,1,0:T(8,128)(2,1)} %bitcast.7, f32[256,128]{1,0:T(8,128)} %draw.1, s32[256]{0:T(256)} %counts.1), custom_call_target="tpu_custom_call" | custom-call | tf_op jit(solution)/shard_map/pallas_call | solution.py:534
  94.6 0.7 copy.8
